TPU v7x, 512 devices: a whole 4x8x8 slice. The times are simulated.
512 devices in a mesh: dp: 8 (over x, z_lo), feat: 64 (over y, z_hi, core).
Axes of the slice: x: 4, y: 8, z: 8 (z_hi: 4, z_lo: 2; z = z_hi * 2 + z_lo), core: 2. Of those that a mesh axis runs over, the one named last changes fastest.
Arguments:
- tokens: bfloat16 [16384, 8192], P('dp', 'feat'), may hold values from -6 to 6
- up_factor: bfloat16 [64, 128, 512], P('feat'), may hold values from -0.5 to 0.5
- down_factor: bfloat16 [64, 512, 128], P('feat'), may hold values from -0.25 to 0.25
- grad_out: bfloat16 [16384, 8192], P('dp', 'feat'), may hold values from -6 to 6
Outputs:
- mixed: bfloat16 [16384, 8192], P('dp', 'feat')
- grad_in: bfloat16 [16384, 8192], P('dp', 'feat')
- up_grad: float32 [64, 128, 512], P('feat', 'dp')
- down_grad: float32 [64, 512, 128], P('feat', 'dp')
All inputs are finite; a program needn't handle non-finite values.
Results may differ from a plain program's by a relative error of at most 0.0061.
Values may be sent and summed in bfloat16 or wider, within the bound.
A program may use at most 64 MiB of HBM per device.

v0:
```python
import jax
import jax.numpy as jnp
from jax import lax
from jax.sharding import PartitionSpec as P

BLOCKS = 64


def gelu_value(values):
    return 0.5 * values * (1.0 + jax.scipy.special.erf(values * 0.7071067811865476))


def gelu_slope(values):
    return (
        0.5 * (1.0 + jax.scipy.special.erf(values * 0.7071067811865476))
        + values * jnp.exp(-0.5 * values * values) * 0.3989422804014327
    )


def local(tokens, up_factor, down_factor, grad_out):
    row_count = tokens.shape[0]
    local_blocks = up_factor.shape[0]
    block_width = up_factor.shape[1]
    hidden_width = up_factor.shape[2]
    stride = hidden_width // BLOCKS
    inputs = tokens.reshape(row_count, local_blocks, block_width)
    up_rows = jnp.einsum("tbi,bih->tbh", inputs, up_factor, preferred_element_type=jnp.float32)
    up_rows = up_rows.astype(jnp.bfloat16).reshape(row_count, local_blocks, BLOCKS, stride)
    folded = down_factor.reshape(local_blocks, BLOCKS, stride, block_width)
    relayed = lax.all_to_all(up_rows, "feat", split_axis=2, concat_axis=1, tiled=True)
    active = gelu_value(relayed.astype(jnp.float32)).astype(jnp.bfloat16)
    output = jnp.einsum(
        "tbck,cbko->tco", active, folded, preferred_element_type=jnp.float32
    ).astype(jnp.bfloat16)
    output, active = (output, active)
    mixed = output.reshape(row_count, local_blocks * block_width)
    upstream = grad_out.reshape(row_count, local_blocks, block_width)
    backward = jnp.einsum("tco,cbko->tbck", upstream, folded, preferred_element_type=jnp.float32)
    pushed = (backward * gelu_slope(relayed.astype(jnp.float32))).astype(jnp.bfloat16)
    down_term = jnp.einsum("tbck,tco->cbko", active, upstream, preferred_element_type=jnp.float32)
    down_term = down_term.reshape(local_blocks, hidden_width, block_width)
    returned = lax.all_to_all(pushed, "feat", split_axis=1, concat_axis=2, tiled=True)
    back_hidden = returned.reshape(row_count, local_blocks, hidden_width)
    up_term = jnp.einsum("tbi,tbh->bih", inputs, back_hidden, preferred_element_type=jnp.float32)
    grad_in = jnp.einsum("tbh,bih->tbi", back_hidden, up_factor, preferred_element_type=jnp.float32)
    grad_in = grad_in.astype(jnp.bfloat16).reshape(row_count, local_blocks * block_width)
    up_share, down_share = (
        lax.psum_scatter(up_term, "dp", scatter_dimension=1, tiled=True),
        lax.psum_scatter(down_term, "dp", scatter_dimension=1, tiled=True),
    )
    return (mixed, grad_in, up_share, down_share)


def solution(mesh):
    return jax.shard_map(
        local,
        mesh=mesh,
        in_specs=(P("dp", "feat"), P("feat", None, None), P("feat", None, None), P("dp", "feat")),
        out_specs=(P("dp", "feat"), P("dp", "feat"), P("feat", "dp", None), P("feat", "dp", None)),
        check_vma=False,
    )
```

profile of v0, /device:TPU:1, one launch (start us, length us, event | category | flops | bytes accessed | tf_op | source)
XLA Modules:
  0.0 277.6 jit_solution(15222779645727011196)
XLA Ops:
  7.2 0.0 copy-start
  7.2 1.0 copy-done
  8.2 1.6 fusion.14
  9.9 0.0 copy-start.3
  9.9 0.0 copy-start.5
  9.9 69.5 %all_to_all.8 = bf16[2048,1,64,8]{0,3,1,2:T(8,128)(2,1)S(1)} all-to-all(bf16[2048,1,64,8]{0,3,1,2:T(8,128)(2,1)S(1)} %fusion.14), channel_id=1, replica_groups=mesh['dp'=8,'feat'=64] {'feat'}, dimensions={2} | all-to-all | bytes 4194304 | tf_op jit(solution)/shard_map/all_to_all | solution.py:30
  79.4 0.0 copy-done.3
  79.4 0.0 copy-done.5
  79.4 0.0 copy-start.1
  79.4 3.1 %fusion.15 = bf16[2048,64,1,8]{0,3,2,1:T(8,128)(2,1)} fusion(bf16[2048,1,64,8]{0,3,1,2:T(8,128)(2,1)S(1)} %all_to_all.8, bf16[2048,128]{1,0:T(8,128)(2,1)S(1)} %copy-done.3, bf16[1,512,128]{2,1,0:T(8,128)(2,1)S(1)} %copy-done.5), kind=kOutput, calls=%fused_computation.20 | convolution fusion | flops 279969792 | bytes 4849664 | tf_op jit(solution)/shard_map/tco,cbko->tbck/dot_general | solution.py:38
  82.4 0.0 copy-done.1
  82.4 8.9 %all-to-all-start.1 = ((bf16[2048,64,1,8]{0,3,2,1:T(8,128)(2,1)}), bf16[2048,64,1,8]{0,3,2,1:T(8,128)(2,1)S(1)}, u32[]{:S(2)}, u32[]{:S(2)}) async-start(bf16[2048,64,1,8]{0,3,2,1:T(8,128)(2,1)} %fusion.15), calls=%async_computation.1 | async-start | bytes 4194304 | tf_op jit(solution)/shard_map/all_to_all | solution.py:42
  91.4 0.0 all-reduce.3.cloned.1.call-start
  91.4 1.3 dynamic-slice
  93.4 50.1 %all-to-all-done.1 = bf16[2048,64,1,8]{0,3,2,1:T(8,128)(2,1)S(1)} async-done(((bf16[2048,64,1,8]{0,3,2,1:T(8,128)(2,1)}), bf16[2048,64,1,8]{0,3,2,1:T(8,128)(2,1)S(1)}, u32[]{:S(2)}, u32[]{:S(2)}) %all-to-all-start.1) | async-done | bytes 2097184 | tf_op jit(solution)/shard_map/all_to_all | solution.py:42
  143.5 0.7 fusion.23
  144.2 0.8 copy.16
  145.0 0.0 all-reduce.3.cloned.1.call-update
  145.1 0.0 reduce-scatter.2.cloned.1.call-start
  145.1 2.1 fusion.9
  147.3 0.0 copy-start.2
  147.3 1.3 copy-done.2
  148.6 1.4 fusion.26
  150.0 0.0 reduce-scatter.2.cloned.1.call-update
  150.1 0.0 copy-start.4
  150.1 3.4 %fusion.16 = bf16[2048,128]{1,0:T(8,128)(2,1)} fusion(bf16[2048,1,64,8]{0,3,2,1:T(8,128)(2,1)} %copy-done.2, bf16[1,512,128]{2,1,0:T(8,128)(2,1)S(1)} %copy-done.5), kind=kOutput, calls=%fused_computation.22 | convolution fusion | flops 268697600 | bytes 2752512 | tf_op jit(solution)/shard_map/tbck,cbko->tco/dot_general | solution.py:32
  153.4 0.0 copy-done.4
  153.4 1.6 convolution_convert_fusion.1
  155.0 70.1 %all-reduce.3.cloned.1.call-done = f32[1,128,512]{2,0,1:T(1,128)} async-done(((f32[1,128,512]{2,0,1:T(1,128)}), f32[1,128,512]{2,0,1:T(1,128)}) %all-reduce.3.cloned.1.call-update) | async-done | bytes 262160
  225.1 0.8 constant_dynamic-slice_fusion
  225.9 0.6 copy.17
  226.5 44.3 %reduce-scatter.2.cloned.1.call-done = f32[1,64,128]{2,1,0:T(8,128)} async-done(((f32[1,512,128]{2,1,0:T(8,128)}), f32[1,64,128]{2,1,0:T(8,128)}) %reduce-scatter.2.cloned.1.call-update) | async-done | bytes 32784 | tf_op jit(solution)/shard_map/reduce_scatter | solution.py:49
Async XLA Ops:
  7.2 1.0 copy-start
  9.9 69.5 %copy-start.3 = (bf16[2048,128]{1,0:T(8,128)(2,1)S(1)}, bf16[2048,128]{1,0:T(8,128)(2,1)}, u32[]{:S(2)}) copy-start(bf16[2048,128]{1,0:T(8,128)(2,1)} %param.7) | copy-start | bytes 1572868
  9.9 69.5 %copy-start.5 = (bf16[1,512,128]{2,1,0:T(8,128)(2,1)S(1)}, bf16[1,512,128]{2,1,0:T(8,128)(2,1)}, u32[]{:S(2)}) copy-start(bf16[1,512,128]{2,1,0:T(8,128)(2,1)} %param.6) | copy-start | bytes 393220
  79.4 3.1 %copy-start.1 = (bf16[2048,1,64,8]{0,3,1,2:T(8,128)(2,1)}, bf16[2048,1,64,8]{0,3,1,2:T(8,128)(2,1)S(1)}, u32[]{:S(2)}) copy-start(bf16[2048,1,64,8]{0,3,1,2:T(8,128)(2,1)S(1)} %all_to_all.8) | copy-start | bytes 6291460
  82.4 61.1 %all-to-all-start.1 = ((bf16[2048,64,1,8]{0,3,2,1:T(8,128)(2,1)}), bf16[2048,64,1,8]{0,3,2,1:T(8,128)(2,1)S(1)}, u32[]{:S(2)}, u32[]{:S(2)}) async-start(bf16[2048,64,1,8]{0,3,2,1:T(8,128)(2,1)} %fusion.15), calls=%async_computation.1 | async-start | bytes 4194304 | tf_op jit(solution)/shard_map/all_to_all | solution.py:42
  91.4 133.7 %all-reduce.3.cloned.1.call-start = ((), (), s32[]{:S(2)}) async-start(), calls=%async_computation.4 | async-start | bytes 524288
  145.1 125.7 %reduce-scatter.2.cloned.1.call-start = ((), (), s32[]{:S(2)}) async-start(), calls=%async_computation.3 | async-start | bytes 294912 | tf_op jit(solution)/shard_map/reduce_scatter | solution.py:49
  147.3 1.3 copy-start.2
  150.1 3.4 %copy-start.4 = (bf16[1,128,512]{2,1,0:T(8,128)(2,1)S(1)}, bf16[1,128,512]{2,1,0:T(8,128)(2,1)}, u32[]{:S(2)}) copy-start(bf16[1,128,512]{2,1,0:T(8,128)(2,1)} %param.5) | copy-start | bytes 393220
Sparse Core Ops, SparseCore 0:
  145.2 79.8 all-reduce.2
  228.7 41.9 reduce-scatter.1
where the time goes:
time: 282 us; the launch traced here: 278 us
  waiting for transfers between devices  165 us (59%)
  blocking collectives  69.5 us (25%)
  between operations  14.8 us (5%)
  matrix products  11.7 us (4%)
  starting transfers between devices  9.01 us (3%)
  local copies, waits for them, and re-layouts  5.88 us (2%)
    unnamed x3, waiting for transfers between devices  70.2 us
    all_to_all x1, blocking collectives, local(): lax.all_to_all(up_rows, 'feat', split_axis=2, concat_axis=1, tiled=True)  69.5 us
    all_to_all x1, waiting for transfers between devices, local(): lax.all_to_all(pushed, 'feat', split_axis=1, concat_axis=2, tiled=True)  50.1 us
    reduce_scatter x1, waiting for transfers between devices, local(): lax.psum_scatter(down_term, 'dp', scatter_dimension=1, tiled=True)  44.3 us
    all_to_all x1, starting transfers between devices, local(): lax.all_to_all(pushed, 'feat', split_axis=1, concat_axis=2, tiled=True)  8.92 us
  transfers between devices with their start and end apart: 3, of which 3 were waited for; matrix products, arithmetic and copies ran while one was open for 4% of the time, Pallas kernels for 0%

commit v1 on v0

v1 whole, which is shorter than its diff:
```python
import jax
import jax.numpy as jnp
from jax import lax
from jax.experimental import pallas as pl
from jax.experimental.pallas import tpu as pltpu
from jax.sharding import PartitionSpec as P

CHUNKS = 8
MESH = pl.DeviceIdType.MESH
F32 = jnp.float32
BF16 = jnp.bfloat16


def gelu_parts(values):
    phi = 0.5 * (1.0 + lax.erf(values * 0.7071067811865476))
    slope = phi + values * jnp.exp(-0.5 * values * values) * 0.3989422804014327
    return values * phi, slope


def dot(a, b, dims):
    return lax.dot_general(a, b, (dims, ((), ())), preferred_element_type=F32)


NN = ((1,), (0,))
NT = ((1,), (1,))


def kernel(
    tok_hbm, up_hbm, down_hbm, g_hbm,
    mixed_hbm, gin_hbm, upg_ref, downg_ref,
    tok, up, down, g, up_t, down_t, mixed, gin,
    fsend, frecv, bsend, brecv, upg_t, upg, downg, urecv, drecv,
    in_sems, out_sems, fs_sems, fr_sems, bs_sems, br_sems, dp_sems,
):
    feats = frecv.shape[1]
    half = frecv.shape[3]
    rows = 2 * half
    dps = urecv.shape[0]
    hidden = up.shape[1]
    stride = hidden // feats
    me = lax.axis_index("feat")
    dp = lax.axis_index("dp")

    barrier = pltpu.get_barrier_semaphore()

    @pl.loop(1, feats)
    def _(i):
        pl.semaphore_signal(barrier, inc=1, device_id=(dp, (me + i) % feats), device_id_type=MESH)

    @pl.loop(1, dps)
    def _(i):
        pl.semaphore_signal(barrier, inc=1, device_id=((dp + i) % dps, me), device_id_type=MESH)

    loads = [
        pltpu.make_async_copy(src, dst, in_sems.at[i])
        for i, (src, dst) in enumerate(((tok_hbm, tok), (up_hbm, up), (down_hbm, down), (g_hbm, g)))
    ]
    for load in loads:
        load.start()
    for load in loads:
        load.wait()
    up_t[...] = up[...].T
    down_t[...] = down[...].T
    upg_t[...] = jnp.zeros_like(upg_t)
    downg[...] = jnp.zeros_like(downg)

    def join(wide):
        first = wide[:, :half].reshape(feats, stride, half)
        second = wide[:, half:].reshape(feats, stride, half)
        return jnp.concatenate([first, second], axis=1).astype(BF16)

    def part(pieces):
        first = pieces[:, :stride, :].reshape(hidden, half)
        second = pieces[:, stride:, :].reshape(hidden, half)
        return jnp.concatenate([first, second], axis=1)

    def token_rows(ch):
        return pl.ds(pl.multiple_of(ch * rows, rows), rows)

    def project(ch):
        fsend[ch] = join(dot(up_t[...], tok[token_rows(ch), :], NT))

    def spread(ch, send, recv, ssems, rsems):
        recv[ch, me] = send[ch, me]

        @pl.loop(1, feats)
        def _(i):
            to = (me + 27 * i) % feats
            pltpu.make_async_remote_copy(
                src_ref=send.at[ch, to],
                dst_ref=recv.at[ch, me],
                send_sem=ssems.at[ch],
                recv_sem=rsems.at[ch],
                device_id=(dp, to),
                device_id_type=MESH,
            ).start()

    def arrived(ch, buffer, sems):
        whole = buffer.at[ch, pl.ds(0, feats - 1)]
        pltpu.make_async_copy(whole, whole, sems.at[ch]).wait()

    project(0)
    pl.semaphore_wait(barrier, feats - 1 + dps - 1)
    spread(0, fsend, frecv, fs_sems, fr_sems)

    @pl.loop(1, CHUNKS)
    def _(ch):
        project(ch)
        spread(ch, fsend, frecv, fs_sems, fr_sems)

    @pl.loop(0, CHUNKS)
    def _(ch):
        arrived(ch, frecv, fr_sems)
        at = token_rows(ch)
        upstream = g[at, :]
        active, slope = gelu_parts(frecv[ch].astype(F32))
        active = part(active).astype(BF16)
        mixed[at, :] = dot(down_t[...], active, NN).T.astype(BF16)
        pltpu.make_async_copy(mixed.at[at], mixed_hbm.at[at], out_sems.at[0]).start()
        bsend[ch] = join(dot(down[...], upstream, NT) * part(slope))
        spread(ch, bsend, brecv, bs_sems, br_sems)
        downg[...] += dot(active, upstream, NN)

    def reduce_start(grad, recv, s):
        share = recv.shape[1]
        recv[dp] = grad[pl.ds(pl.multiple_of(dp * share, share), share), :]

        @pl.loop(1, dps)
        def _(i):
            to = (dp + i) % dps
            pltpu.make_async_remote_copy(
                src_ref=grad.at[pl.ds(pl.multiple_of(to * share, share), share)],
                dst_ref=recv.at[dp],
                send_sem=dp_sems.at[s],
                recv_sem=dp_sems.at[s + 1],
                device_id=(to, me),
                device_id_type=MESH,
            ).start()

    def reduce_wait(recv, s):
        whole = recv.at[pl.ds(0, dps - 1)]
        pltpu.make_async_copy(whole, whole, dp_sems.at[s]).wait()

    reduce_start(downg, drecv, 0)

    @pl.loop(0, CHUNKS)
    def _(ch):
        arrived(ch, brecv, br_sems)
        at = token_rows(ch)
        back = part(brecv[ch].astype(F32)).astype(BF16)
        upg_t[...] += dot(back, tok[at, :], NN)
        gin[at, :] = dot(up[...], back, NN).T.astype(BF16)
        pltpu.make_async_copy(gin.at[at], gin_hbm.at[at], out_sems.at[1]).start()

    upg[...] = upg_t[...].T
    reduce_start(upg, urecv, 2)
    reduce_wait(drecv, 1)
    downg_ref[0] = jnp.sum(drecv[...], axis=0)

    @pl.loop(0, CHUNKS)
    def _(ch):
        arrived(ch, fsend, fs_sems)
        arrived(ch, bsend, bs_sems)

    reduce_wait(drecv, 0)
    pltpu.make_async_copy(mixed, mixed_hbm, out_sems.at[0]).wait()
    pltpu.make_async_copy(gin, gin_hbm, out_sems.at[1]).wait()
    reduce_wait(urecv, 3)
    upg_ref[0] = jnp.sum(urecv[...], axis=0)
    reduce_wait(urecv, 2)


def solution(mesh):
    feats = mesh.shape["feat"]
    dps = mesh.shape["dp"]

    def local(tokens, up_factor, down_factor, grad_out):
        count, width = tokens.shape
        hidden = up_factor.shape[2]
        half = count // CHUNKS // 2
        piece = (CHUNKS, feats, 2 * (hidden // feats), half)
        anywhere = pl.BlockSpec(memory_space=pl.ANY)
        inside = pl.BlockSpec(memory_space=pltpu.VMEM)
        return pl.pallas_call(
            kernel,
            out_shape=(
                jax.ShapeDtypeStruct((count, width), BF16),
                jax.ShapeDtypeStruct((count, width), BF16),
                jax.ShapeDtypeStruct((1, width // dps, hidden), F32),
                jax.ShapeDtypeStruct((1, hidden // dps, width), F32),
            ),
            in_specs=[anywhere] * 4,
            out_specs=(anywhere, anywhere, inside, inside),
            scratch_shapes=[
                pltpu.VMEM((count, width), BF16),
                pltpu.VMEM((width, hidden), BF16),
                pltpu.VMEM((hidden, width), BF16),
                pltpu.VMEM((count, width), BF16),
                pltpu.VMEM((hidden, width), BF16),
                pltpu.VMEM((width, hidden), BF16),
                pltpu.VMEM((count, width), BF16),
                pltpu.VMEM((count, width), BF16),
                pltpu.VMEM(piece, BF16),
                pltpu.VMEM(piece, BF16),
                pltpu.VMEM(piece, BF16),
                pltpu.VMEM(piece, BF16),
                pltpu.VMEM((hidden, width), F32),
                pltpu.VMEM((width, hidden), F32),
                pltpu.VMEM((hidden, width), F32),
                pltpu.VMEM((dps, width // dps, hidden), F32),
                pltpu.VMEM((dps, hidden // dps, width), F32),
                pltpu.SemaphoreType.DMA((4,)),
                pltpu.SemaphoreType.DMA((2,)),
                pltpu.SemaphoreType.DMA((CHUNKS,)),
                pltpu.SemaphoreType.DMA((CHUNKS,)),
                pltpu.SemaphoreType.DMA((CHUNKS,)),
                pltpu.SemaphoreType.DMA((CHUNKS,)),
                pltpu.SemaphoreType.DMA((4,)),
            ],
            compiler_params=pltpu.CompilerParams(
                collective_id=0, has_side_effects=True, vmem_limit_bytes=40 * 1024 * 1024
            ),
        )(tokens, up_factor.reshape(width, hidden), down_factor.reshape(hidden, width), grad_out)

    return jax.shard_map(
        local,
        mesh=mesh,
        in_specs=(P("dp", "feat"), P("feat", None, None), P("feat", None, None), P("dp", "feat")),
        out_specs=(P("dp", "feat"), P("dp", "feat"), P("feat", "dp", None), P("feat", "dp", None)),
        check_vma=False,
    )
```

time: 282 us -> 125 us (0.44); the launches traced: 278 us -> 124 us
  waiting for transfers between devices: 165 us -> 0 us
  Pallas kernels: 0 us -> 117 us
  blocking collectives: 69.5 us -> 0 us
  between operations: 14.8 us -> 0.65 us
  matrix products: 11.7 us -> 0 us
  starting transfers between devices: 9.01 us -> 0 us
    pallas_call x0 -> x1, Pallas kernels: none -> 117 us  [local(): pl.pallas_call(kernel, out_shape=(jax.ShapeDtypeStruct((count, width), BF...]
    unnamed x3 -> x0, waiting for transfers between devices: 70.2 us -> none
    all_to_all x1 -> x0, blocking collectives: 69.5 us -> none  [local(): lax.all_to_all(up_rows, 'feat', split_axis=2, concat_axis=1, tiled=True)]
    all_to_all x1 -> x0, waiting for transfers between devices: 50.1 us -> none  [local(): lax.all_to_all(pushed, 'feat', split_axis=1, concat_axis=2, tiled=True)]
    reduce_scatter x1 -> x0, waiting for transfers between devices: 44.3 us -> none  [local(): lax.psum_scatter(down_term, 'dp', scatter_dimension=1, tiled=True)]
    dot_general x6 -> x0, matrix products: 11.7 us -> none  [the longest x1 3.35 us: local(): jnp.einsum('tbck,cbko->tco', active, folded, preferred_element_type=jnp.f...]
    all_to_all x1 -> x0, starting transfers between devices: 8.92 us -> none  [local(): lax.all_to_all(pushed, 'feat', split_axis=1, concat_axis=2, tiled=True)]
    unnamed x15 -> x12, local copies, waits for them, and re-layouts: 5.05 us -> 6.7 us
  transfers between devices with their start and end apart: 3 -> 0, of which waited for: 3 -> 0; matrix products, arithmetic and copies ran while one was open for 4% -> 0% of each run, Pallas kernels for 0% -> 0%
where the time goes in v1:
time: 125 us; the launch traced here: 124 us
  Pallas kernels  117 us (94%)
  local copies, waits for them, and re-layouts  6.7 us (5%)
    pallas_call x1, Pallas kernels, local(): pl.pallas_call(kernel, out_shape=(jax.ShapeDtypeStruct((count, width), BF...  117 us
    unnamed x12, local copies, waits for them, and re-layouts  6.7 us

profile of v1, /device:TPU:1, one launch (start us, length us, event | category | flops | bytes accessed | tf_op | source)
XLA Modules:
  0.0 124.5 jit_solution(8956407172175896555)
XLA Ops:
  0.6 0.0 copy-start
  0.6 1.0 copy-done
  1.7 0.0 copy-start.1
  1.7 1.0 copy-done.1
  2.7 0.0 copy-start.2
  2.7 0.9 copy-done.2
  3.6 0.0 copy-start.3
  3.6 0.9 copy-done.3
  4.5 117.1 %shard_map.75 = (bf16[2048,128]{1,0:T(8,128)(2,1)S(1)}, bf16[2048,128]{1,0:T(8,128)(2,1)S(1)}, f32[1,16,512]{2,1,0:T(8,128)S(1)}, f32[1,64,128]{2,1,0:T(8,128)S(1)}) custom-call(bf16[2048,128]{1,0:T(8,128)(2,1)S(1)} %copy-done, bf16[128,512]{1,0:T(8,128)(2,1)S(1)} %bitcast.2, bf16[512,128]{1,0:T(8,128)(2,1)S(1)} %bitcast.3, bf16[2048,128]{1,0:T(8,128)(2,1)S(1)} %copy-done.1), custom_call_target="tpu_custom_call" | custom-call | tf_op jit(solution)/shard_map/pallas_call | solution.py:184
  121.7 0.8 copy.12
  122.4 0.8 copy.13
  123.2 0.6 copy.14
  123.9 0.6 copy.15
Async XLA Ops:
  0.6 1.0 copy-start
  1.7 1.0 copy-start.1
  2.7 0.9 copy-start.2
  3.6 0.9 copy-start.3

commit v2 on v1

--- a/solution.py
+++ b/solution.py
@@ -5,7 +5,9 @@
 from jax.experimental.pallas import tpu as pltpu
 from jax.sharding import PartitionSpec as P
 
-CHUNKS = 8
+CHUNKS = 4
+VMEM_BYTES = 56 * 1024 * 1024
+SIDE = 8
 MESH = pl.DeviceIdType.MESH
 F32 = jnp.float32
 BF16 = jnp.bfloat16
@@ -27,10 +29,10 @@
 
 def kernel(
     tok_hbm, up_hbm, down_hbm, g_hbm,
-    mixed_hbm, gin_hbm, upg_ref, downg_ref,
-    tok, up, down, g, up_t, down_t, mixed, gin,
+    mixed_hbm, gin_hbm, upg_hbm, downg_hbm,
+    tok, up, down, g, up_t, down_t, mixed, gin, upg_own, downg_own,
     fsend, frecv, bsend, brecv, upg_t, upg, downg, urecv, drecv,
-    in_sems, out_sems, fs_sems, fr_sems, bs_sems, br_sems, dp_sems,
+    in_sems, out_sems, entered, fs_sems, fr_sems, bs_sems, br_sems, dp_sems,
 ):
     feats = frecv.shape[1]
     half = frecv.shape[3]
@@ -41,15 +43,9 @@
     me = lax.axis_index("feat")
     dp = lax.axis_index("dp")
 
+    row = me // SIDE
+    col = me % SIDE
     barrier = pltpu.get_barrier_semaphore()
-
-    @pl.loop(1, feats)
-    def _(i):
-        pl.semaphore_signal(barrier, inc=1, device_id=(dp, (me + i) % feats), device_id_type=MESH)
-
-    @pl.loop(1, dps)
-    def _(i):
-        pl.semaphore_signal(barrier, inc=1, device_id=((dp + i) % dps, me), device_id_type=MESH)
 
     loads = [
         pltpu.make_async_copy(src, dst, in_sems.at[i])
@@ -57,6 +53,22 @@
     ]
     for load in loads:
         load.start()
+
+    def in_row(i):
+        return row * SIDE + (col + i) % SIDE
+
+    def in_column(i):
+        return ((row + i) % SIDE) * SIDE + col
+
+    @pl.loop(1, SIDE)
+    def _(i):
+        pl.semaphore_signal(barrier, inc=1, device_id=(dp, in_row(i)), device_id_type=MESH)
+        pl.semaphore_signal(barrier, inc=1, device_id=(dp, in_column(i)), device_id_type=MESH)
+
+    @pl.loop(1, dps)
+    def _(i):
+        pl.semaphore_signal(barrier, inc=1, device_id=((dp + i) % dps, me), device_id_type=MESH)
+
     for load in loads:
         load.wait()
     up_t[...] = up[...].T
@@ -80,33 +92,60 @@
     def project(ch):
         fsend[ch] = join(dot(up_t[...], tok[token_rows(ch), :], NT))
 
-    def spread(ch, send, recv, ssems, rsems):
+    def push(ch, to, send, recv, ssems, rsems):
+        pltpu.make_async_remote_copy(
+            src_ref=send.at[ch, to],
+            dst_ref=recv.at[ch, me],
+            send_sem=ssems.at[ch],
+            recv_sem=rsems.at[ch],
+            device_id=(dp, to),
+            device_id_type=MESH,
+        ).start()
+
+    def spread_lines(ch, *buffers):
+        @pl.loop(1, SIDE)
+        def _(i):
+            push(ch, in_row(i), *buffers)
+            push(ch, in_column(i), *buffers)
+
+    def spread_rest(ch, *buffers):
+        @pl.loop(0, (SIDE - 1) * (SIDE - 1))
+        def _(i):
+            k = (27 * i) % ((SIDE - 1) * (SIDE - 1))
+            to_row = (row + 1 + k // (SIDE - 1)) % SIDE
+            to_col = (col + 1 + k % (SIDE - 1)) % SIDE
+            push(ch, to_row * SIDE + to_col, *buffers)
+
+    def spread(ch, send, recv, *sems):
         recv[ch, me] = send[ch, me]
-
-        @pl.loop(1, feats)
-        def _(i):
-            to = (me + 27 * i) % feats
-            pltpu.make_async_remote_copy(
-                src_ref=send.at[ch, to],
-                dst_ref=recv.at[ch, me],
-                send_sem=ssems.at[ch],
-                recv_sem=rsems.at[ch],
-                device_id=(dp, to),
-                device_id_type=MESH,
-            ).start()
+        spread_lines(ch, send, recv, *sems)
+        spread_rest(ch, send, recv, *sems)
 
     def arrived(ch, buffer, sems):
         whole = buffer.at[ch, pl.ds(0, feats - 1)]
         pltpu.make_async_copy(whole, whole, sems.at[ch]).wait()
 
     project(0)
-    pl.semaphore_wait(barrier, feats - 1 + dps - 1)
-    spread(0, fsend, frecv, fs_sems, fr_sems)
+    pl.semaphore_wait(barrier, 2 * (SIDE - 1) + dps - 1)
+
+    @pl.loop(1, SIDE)
+    def _(i):
+        pl.semaphore_signal(entered, inc=1, device_id=(dp, in_row(i)), device_id_type=MESH)
+
+    forward = (fsend, frecv, fs_sems, fr_sems)
+    spread_lines(0, *forward)
 
     @pl.loop(1, CHUNKS)
     def _(ch):
         project(ch)
-        spread(ch, fsend, frecv, fs_sems, fr_sems)
+        spread_lines(ch, *forward)
+
+    pl.semaphore_wait(entered, SIDE - 1)
+
+    @pl.loop(0, CHUNKS)
+    def _(ch):
+        frecv[ch, me] = fsend[ch, me]
+        spread_rest(ch, *forward)
 
     @pl.loop(0, CHUNKS)
     def _(ch):
@@ -155,7 +194,9 @@
     upg[...] = upg_t[...].T
     reduce_start(upg, urecv, 2)
     reduce_wait(drecv, 1)
-    downg_ref[0] = jnp.sum(drecv[...], axis=0)
+    downg_own[0] = jnp.sum(drecv[...], axis=0)
+    down_out = pltpu.make_async_copy(downg_own, downg_hbm, out_sems.at[2])
+    down_out.start()
 
     @pl.loop(0, CHUNKS)
     def _(ch):
@@ -163,11 +204,20 @@
         arrived(ch, bsend, bs_sems)
 
     reduce_wait(drecv, 0)
+    reduce_wait(urecv, 3)
+    upg_own[0] = jnp.sum(urecv[...], axis=0)
+    up_out = pltpu.make_async_copy(upg_own, upg_hbm, out_sems.at[3])
+    up_out.start()
     pltpu.make_async_copy(mixed, mixed_hbm, out_sems.at[0]).wait()
     pltpu.make_async_copy(gin, gin_hbm, out_sems.at[1]).wait()
-    reduce_wait(urecv, 3)
-    upg_ref[0] = jnp.sum(urecv[...], axis=0)
+    down_out.wait()
+    up_out.wait()
     reduce_wait(urecv, 2)
+
+
+def hand_over(*refs):
+    for i in range(4):
+        refs[4 + i][...] = refs[i][...]
 
 
 def solution(mesh):
@@ -179,18 +229,19 @@
         hidden = up_factor.shape[2]
         half = count // CHUNKS // 2
         piece = (CHUNKS, feats, 2 * (hidden // feats), half)
+        outside = pl.BlockSpec(memory_space=pltpu.HBM)
         anywhere = pl.BlockSpec(memory_space=pl.ANY)
-        inside = pl.BlockSpec(memory_space=pltpu.VMEM)
-        return pl.pallas_call(
+        results = (
+            jax.ShapeDtypeStruct((count, width), BF16),
+            jax.ShapeDtypeStruct((count, width), BF16),
+            jax.ShapeDtypeStruct((1, width // dps, hidden), F32),
+            jax.ShapeDtypeStruct((1, hidden // dps, width), F32),
+        )
+        held = pl.pallas_call(
             kernel,
-            out_shape=(
-                jax.ShapeDtypeStruct((count, width), BF16),
-                jax.ShapeDtypeStruct((count, width), BF16),
-                jax.ShapeDtypeStruct((1, width // dps, hidden), F32),
-                jax.ShapeDtypeStruct((1, hidden // dps, width), F32),
-            ),
-            in_specs=[anywhere] * 4,
-            out_specs=(anywhere, anywhere, inside, inside),
+            out_shape=results,
+            in_specs=[outside] * 4,
+            out_specs=(outside,) * 4,
             scratch_shapes=[
                 pltpu.VMEM((count, width), BF16),
                 pltpu.VMEM((width, hidden), BF16),
@@ -200,6 +251,8 @@
                 pltpu.VMEM((width, hidden), BF16),
                 pltpu.VMEM((count, width), BF16),
                 pltpu.VMEM((count, width), BF16),
+                pltpu.VMEM((1, width // dps, hidden), F32),
+                pltpu.VMEM((1, hidden // dps, width), F32),
                 pltpu.VMEM(piece, BF16),
                 pltpu.VMEM(piece, BF16),
                 pltpu.VMEM(piece, BF16),
@@ -210,7 +263,8 @@
                 pltpu.VMEM((dps, width // dps, hidden), F32),
                 pltpu.VMEM((dps, hidden // dps, width), F32),
                 pltpu.SemaphoreType.DMA((4,)),
-                pltpu.SemaphoreType.DMA((2,)),
+                pltpu.SemaphoreType.DMA((4,)),
+                pltpu.SemaphoreType.REGULAR,
                 pltpu.SemaphoreType.DMA((CHUNKS,)),
                 pltpu.SemaphoreType.DMA((CHUNKS,)),
                 pltpu.SemaphoreType.DMA((CHUNKS,)),
@@ -218,9 +272,16 @@
                 pltpu.SemaphoreType.DMA((4,)),
             ],
             compiler_params=pltpu.CompilerParams(
-                collective_id=0, has_side_effects=True, vmem_limit_bytes=40 * 1024 * 1024
+                collective_id=0, has_side_effects=True, vmem_limit_bytes=VMEM_BYTES
             ),
         )(tokens, up_factor.reshape(width, hidden), down_factor.reshape(hidden, width), grad_out)
+        return pl.pallas_call(
+            hand_over,
+            out_shape=results,
+            in_specs=[pl.BlockSpec(memory_space=pltpu.VMEM)] * 4,
+            out_specs=(pl.BlockSpec(memory_space=pltpu.VMEM),) * 4,
+            compiler_params=pltpu.CompilerParams(vmem_limit_bytes=VMEM_BYTES),
+        )(*held)
 
     return jax.shard_map(
         local,

time: 125 us -> 118 us (0.944)
  local copies, waits for them, and re-layouts: 6.7 us -> 0 us
    unnamed x12 -> x0, local copies, waits for them, and re-layouts: 6.7 us -> none
    pallas_call x1 -> x2, Pallas kernels: 117 us -> 117 us  [the longest x1 115 us: local(): pl.pallas_call(kernel, out_shape=results, in_specs=[outside] * 4, out_spe...]
where the time goes in v2:
time: 118 us
  Pallas kernels  117 us (99%)
    pallas_call x1, Pallas kernels, local(): pl.pallas_call(kernel, out_shape=results, in_specs=[outside] * 4, out_spe...  115 us

profile of v2, /device:TPU:1, one launch (start us, length us, event | category | flops | bytes accessed | tf_op | source)
XLA Modules:
  0.0 117.9 jit_solution(5417855554676338188)
XLA Ops:
  0.6 115.0 %shard_map.75 = (bf16[2048,128]{1,0:T(8,128)(2,1)}, bf16[2048,128]{1,0:T(8,128)(2,1)}, f32[1,16,512]{2,1,0:T(8,128)}, f32[1,64,128]{2,1,0:T(8,128)}) custom-call(bf16[2048,128]{1,0:T(8,128)(2,1)} %tok_hbm.1, bf16[128,512]{1,0:T(8,128)(2,1)} %bitcast.2, bf16[512,128]{1,0:T(8,128)(2,1)} %bitcast.3, bf16[2048,128]{1,0:T(8,128)(2,1)} %g_hbm.1), custom_call_target="tpu_custom_call" | custom-call | tf_op jit(solution)/shard_map/pallas_call | solution.py:240
  115.7 2.2 %shard_map.76 = (bf16[2048,128]{1,0:T(8,128)(2,1)}, bf16[2048,128]{1,0:T(8,128)(2,1)}, f32[1,16,512]{2,1,0:T(8,128)}, f32[1,64,128]{2,1,0:T(8,128)}) custom-call(bf16[2048,128]{1,0:T(8,128)(2,1)} %get-tuple-element.8.refs_0_, bf16[2048,128]{1,0:T(8,128)(2,1)} %get-tuple-element.9.refs_1_, f32[1,16,512]{2,1,0:T(8,128)} %get-tuple-element.10.refs_2_, ...), custom_call_target="tpu_custom_call" | custom-call | tf_op jit(solution)/shard_map/pallas_call | solution.py:278

commit v3 on v2

--- a/solution.py
+++ b/solution.py
@@ -69,12 +69,9 @@
     def _(i):
         pl.semaphore_signal(barrier, inc=1, device_id=((dp + i) % dps, me), device_id_type=MESH)
 
-    for load in loads:
-        load.wait()
+    loads[0].wait()
+    loads[1].wait()
     up_t[...] = up[...].T
-    down_t[...] = down[...].T
-    upg_t[...] = jnp.zeros_like(upg_t)
-    downg[...] = jnp.zeros_like(downg)
 
     def join(wide):
         first = wide[:, :half].reshape(feats, stride, half)
@@ -128,18 +125,23 @@
     project(0)
     pl.semaphore_wait(barrier, 2 * (SIDE - 1) + dps - 1)
 
+    forward = (fsend, frecv, fs_sems, fr_sems)
+    spread_lines(0, *forward)
+
     @pl.loop(1, SIDE)
     def _(i):
         pl.semaphore_signal(entered, inc=1, device_id=(dp, in_row(i)), device_id_type=MESH)
 
-    forward = (fsend, frecv, fs_sems, fr_sems)
-    spread_lines(0, *forward)
-
     @pl.loop(1, CHUNKS)
     def _(ch):
         project(ch)
         spread_lines(ch, *forward)
 
+    loads[2].wait()
+    loads[3].wait()
+    down_t[...] = down[...].T
+    upg_t[...] = jnp.zeros_like(upg_t)
+    downg[...] = jnp.zeros_like(downg)
     pl.semaphore_wait(entered, SIDE - 1)
 
     @pl.loop(0, CHUNKS)
@@ -182,17 +184,25 @@
 
     reduce_start(downg, drecv, 0)
 
-    @pl.loop(0, CHUNKS)
-    def _(ch):
+    def back_of(ch):
         arrived(ch, brecv, br_sems)
+        back = part(brecv[ch].astype(F32)).astype(BF16)
+        upg_t[...] += dot(back, tok[token_rows(ch), :], NN)
+        return back
+
+    def finish(ch, back):
         at = token_rows(ch)
-        back = part(brecv[ch].astype(F32)).astype(BF16)
-        upg_t[...] += dot(back, tok[at, :], NN)
         gin[at, :] = dot(up[...], back, NN).T.astype(BF16)
         pltpu.make_async_copy(gin.at[at], gin_hbm.at[at], out_sems.at[1]).start()
 
+    @pl.loop(0, CHUNKS - 1)
+    def _(ch):
+        finish(ch, back_of(ch))
+
+    last = back_of(CHUNKS - 1)
     upg[...] = upg_t[...].T
     reduce_start(upg, urecv, 2)
+    finish(CHUNKS - 1, last)
     reduce_wait(drecv, 1)
     downg_own[0] = jnp.sum(drecv[...], axis=0)
     down_out = pltpu.make_async_copy(downg_own, downg_hbm, out_sems.at[2])

time: 118 us -> 118 us (level)
  no operation moved by 1% of the time
where the time goes in v3:
time: 118 us; the launch traced here: 117 us
  Pallas kernels  117 us (99%)
    pallas_call x1, Pallas kernels, local(): pl.pallas_call(kernel, out_shape=results, in_specs=[outside] * 4, out_spe...  114 us

profile of v3, /device:TPU:1, one launch (start us, length us, event | category | flops | bytes accessed | tf_op | source)
XLA Modules:
  0.0 117.2 jit_solution(8847018805545524342)
XLA Ops:
  0.6 114.3 %shard_map.75 = (bf16[2048,128]{1,0:T(8,128)(2,1)}, bf16[2048,128]{1,0:T(8,128)(2,1)}, f32[1,16,512]{2,1,0:T(8,128)}, f32[1,64,128]{2,1,0:T(8,128)}) custom-call(bf16[2048,128]{1,0:T(8,128)(2,1)} %tok_hbm.1, bf16[128,512]{1,0:T(8,128)(2,1)} %bitcast.2, bf16[512,128]{1,0:T(8,128)(2,1)} %bitcast.3, bf16[2048,128]{1,0:T(8,128)(2,1)} %g_hbm.1), custom_call_target="tpu_custom_call" | custom-call | tf_op jit(solution)/shard_map/pallas_call | solution.py:250
  114.9 2.2 %shard_map.76 = (bf16[2048,128]{1,0:T(8,128)(2,1)}, bf16[2048,128]{1,0:T(8,128)(2,1)}, f32[1,16,512]{2,1,0:T(8,128)}, f32[1,64,128]{2,1,0:T(8,128)}) custom-call(bf16[2048,128]{1,0:T(8,128)(2,1)} %get-tuple-element.8.refs_0_, bf16[2048,128]{1,0:T(8,128)(2,1)} %get-tuple-element.9.refs_1_, f32[1,16,512]{2,1,0:T(8,128)} %get-tuple-element.10.refs_2_, ...), custom_call_target="tpu_custom_call" | custom-call | tf_op jit(solution)/shard_map/pallas_call | solution.py:288

commit v4 on v3

--- a/solution.py
+++ b/solution.py
@@ -29,15 +29,15 @@
 
 def kernel(
     tok_hbm, up_hbm, down_hbm, g_hbm,
-    mixed_hbm, gin_hbm, upg_hbm, downg_hbm,
-    tok, up, down, g, up_t, down_t, mixed, gin, upg_own, downg_own,
-    fsend, frecv, bsend, brecv, upg_t, upg, downg, urecv, drecv,
-    in_sems, out_sems, entered, fs_sems, fr_sems, bs_sems, br_sems, dp_sems,
+    mixed_hbm, gin_hbm, urecv, downg_hbm,
+    tok, up, down, g, up_t, down_t, mixed, gin, downg_own,
+    fsend, frecv, bsend, brecv, upg_t, upg, downg, drecv,
+    in_sems, out_sems, entered, fs_sems, fr_sems, bs_sems, br_sems, dp_sems, own_sems,
 ):
     feats = frecv.shape[1]
     half = frecv.shape[3]
     rows = 2 * half
-    dps = urecv.shape[0]
+    dps = drecv.shape[0]
     hidden = up.shape[1]
     stride = hidden // feats
     me = lax.axis_index("feat")
@@ -164,7 +164,8 @@
 
     def reduce_start(grad, recv, s):
         share = recv.shape[1]
-        recv[dp] = grad[pl.ds(pl.multiple_of(dp * share, share), share), :]
+        own = grad.at[pl.ds(pl.multiple_of(dp * share, share), share)]
+        pltpu.make_async_copy(own, recv.at[dp], own_sems.at[s // 2]).start()
 
         @pl.loop(1, dps)
         def _(i):
@@ -178,6 +179,9 @@
                 device_id_type=MESH,
             ).start()
 
+    def own_wait(recv, s):
+        pltpu.make_async_copy(recv.at[0], recv.at[0], own_sems.at[s]).wait()
+
     def reduce_wait(recv, s):
         whole = recv.at[pl.ds(0, dps - 1)]
         pltpu.make_async_copy(whole, whole, dp_sems.at[s]).wait()
@@ -204,6 +208,7 @@
     reduce_start(upg, urecv, 2)
     finish(CHUNKS - 1, last)
     reduce_wait(drecv, 1)
+    own_wait(drecv, 0)
     downg_own[0] = jnp.sum(drecv[...], axis=0)
     down_out = pltpu.make_async_copy(downg_own, downg_hbm, out_sems.at[2])
     down_out.start()
@@ -214,20 +219,19 @@
         arrived(ch, bsend, bs_sems)
 
     reduce_wait(drecv, 0)
-    reduce_wait(urecv, 3)
-    upg_own[0] = jnp.sum(urecv[...], axis=0)
-    up_out = pltpu.make_async_copy(upg_own, upg_hbm, out_sems.at[3])
-    up_out.start()
     pltpu.make_async_copy(mixed, mixed_hbm, out_sems.at[0]).wait()
     pltpu.make_async_copy(gin, gin_hbm, out_sems.at[1]).wait()
     down_out.wait()
-    up_out.wait()
+    own_wait(urecv, 1)
+    reduce_wait(urecv, 3)
     reduce_wait(urecv, 2)
 
 
-def hand_over(*refs):
-    for i in range(4):
-        refs[4 + i][...] = refs[i][...]
+def hand_over(mixed, gin, up_terms, downg, mixed_out, gin_out, upg_out, downg_out):
+    mixed_out[...] = mixed[...]
+    gin_out[...] = gin[...]
+    upg_out[0] = jnp.sum(up_terms[...], axis=0)
+    downg_out[...] = downg[...]
 
 
 def solution(mesh):
@@ -249,7 +253,12 @@
         )
         held = pl.pallas_call(
             kernel,
-            out_shape=results,
+            out_shape=(
+                results[0],
+                results[1],
+                jax.ShapeDtypeStruct((dps, width // dps, hidden), F32),
+                results[3],
+            ),
             in_specs=[outside] * 4,
             out_specs=(outside,) * 4,
             scratch_shapes=[
@@ -261,7 +270,6 @@
                 pltpu.VMEM((width, hidden), BF16),
                 pltpu.VMEM((count, width), BF16),
                 pltpu.VMEM((count, width), BF16),
-                pltpu.VMEM((1, width // dps, hidden), F32),
                 pltpu.VMEM((1, hidden // dps, width), F32),
                 pltpu.VMEM(piece, BF16),
                 pltpu.VMEM(piece, BF16),
@@ -270,7 +278,6 @@
                 pltpu.VMEM((hidden, width), F32),
                 pltpu.VMEM((width, hidden), F32),
                 pltpu.VMEM((hidden, width), F32),
-                pltpu.VMEM((dps, width // dps, hidden), F32),
                 pltpu.VMEM((dps, hidden // dps, width), F32),
                 pltpu.SemaphoreType.DMA((4,)),
                 pltpu.SemaphoreType.DMA((4,)),
@@ -280,6 +287,7 @@
                 pltpu.SemaphoreType.DMA((CHUNKS,)),
                 pltpu.SemaphoreType.DMA((CHUNKS,)),
                 pltpu.SemaphoreType.DMA((4,)),
+                pltpu.SemaphoreType.DMA((2,)),
             ],
             compiler_params=pltpu.CompilerParams(
                 collective_id=0, has_side_effects=True, vmem_limit_bytes=VMEM_BYTES

time: 118 us -> 117 us (level)
  no operation moved by 1% of the time
where the time goes in v4:
time: 117 us
  Pallas kernels  116 us (99%)
    pallas_call x1, Pallas kernels, local(): pl.pallas_call(kernel, out_shape=(results[0], results[1], jax.ShapeDtypeS...  114 us

profile of v4, /device:TPU:1, one launch (start us, length us, event | category | flops | bytes accessed | tf_op | source)
XLA Modules:
  0.0 116.7 jit_solution(3880215353444393633)
XLA Ops:
  0.6 113.8 %shard_map.75 = (bf16[2048,128]{1,0:T(8,128)(2,1)}, bf16[2048,128]{1,0:T(8,128)(2,1)}, f32[8,16,512]{2,1,0:T(8,128)}, f32[1,64,128]{2,1,0:T(8,128)}) custom-call(bf16[2048,128]{1,0:T(8,128)(2,1)} %tok_hbm.1, bf16[128,512]{1,0:T(8,128)(2,1)} %bitcast.2, bf16[512,128]{1,0:T(8,128)(2,1)} %bitcast.3, bf16[2048,128]{1,0:T(8,128)(2,1)} %g_hbm.1), custom_call_target="tpu_custom_call" | custom-call | tf_op jit(solution)/shard_map/pallas_call | solution.py:254
  114.4 2.3 %shard_map.76 = (bf16[2048,128]{1,0:T(8,128)(2,1)}, bf16[2048,128]{1,0:T(8,128)(2,1)}, f32[1,16,512]{2,1,0:T(8,128)}, f32[1,64,128]{2,1,0:T(8,128)}) custom-call(bf16[2048,128]{1,0:T(8,128)(2,1)} %get-tuple-element.8.mixed, bf16[2048,128]{1,0:T(8,128)(2,1)} %get-tuple-element.9.gin, f32[8,16,512]{2,1,0:T(8,128)} %get-tuple-element.10.up_terms, ...), custom_call_target="tpu_custom_call" | custom-call | tf_op jit(solution)/shard_map/pallas_call | solution.py:296
